TPU v7x, 32 devices: a whole 2x2x4 slice. The times are simulated.
32 devices in a mesh: dp: 4 (over y, x), ctx: 4 (over z), tensor: 2 (over core).
Axes of the slice: x: 2, y: 2, z: 4, core: 2. Of those that a mesh axis runs over, the one named last changes fastest.
Arguments:
- inputs: float32 [4, 4096, 768], P('dp', 'ctx', 'tensor'), may hold values from -6 to 6
- out_grad: float32 [4, 4096, 768], P('dp', 'ctx', 'tensor'), may hold values from -6 to 6
- attn_gain: float32 [768], P('tensor'), may hold values from 0.5 to 1.5
- query_key_value_weight: float32 [768, 3, 768], P(None, None, 'tensor'), may hold values from -0.21875 to 0.21875
- attention_output_weight: float32 [768, 768], P('tensor'), may hold values from -1.75 to 1.75
- mlp_gain: float32 [768], P('tensor'), may hold values from 0.5 to 1.5
- feedforward_input_weight: float32 [768, 2, 1152], P(None, None, 'tensor'), may hold values from -0.21875 to 0.21875
- feedforward_output_weight: float32 [1152, 768], P('tensor'), may hold values from -0.1875 to 0.1875
Outputs:
- layer_out: float32 [4, 4096, 768], P('dp', 'ctx', 'tensor')
- input_grad: float32 [4, 4096, 768], P('dp', 'ctx', 'tensor')
- attn_gain_grad: float32 [768], P('tensor')
- qkv_grad: float32 [768, 3, 768], P(None, None, 'tensor')
- attn_out_grad: float32 [768, 768], P('tensor')
- mlp_gain_grad: float32 [768], P('tensor')
- mlp_in_grad: float32 [768, 2, 1152], P(None, None, 'tensor')
- mlp_out_grad: float32 [1152, 768], P('tensor')
All inputs are finite; a program needn't handle non-finite values.
Results may differ from a plain program's by a relative error of at most 0.0003.
Values sent between devices are 32-bit elements; how exact they have to be, the bound alone decides.
A program may use at most 256 MiB of HBM per device.

v0:
```python
import jax
import jax.numpy as jnp
from jax import lax
from jax.sharding import PartitionSpec as P

D = 768
HEAD_DIM = 64


EPSILON = 1e-05
ROPE_BASE = 160000.0
EXACT_PRECISION = lax.Precision.HIGHEST


def rope_tables(positions):
    half_dim = HEAD_DIM // 2
    frequency = jnp.power(ROPE_BASE, -2.0 * jnp.arange(half_dim, dtype=jnp.float32) / HEAD_DIM)
    angles = positions[:, None] * frequency[None, :]
    cosine = jnp.concatenate([jnp.cos(angles), jnp.cos(angles)], axis=-1)
    sine = jnp.concatenate([jnp.sin(angles), jnp.sin(angles)], axis=-1)
    return (cosine, sine)


def rotate(values, cosine, sine):
    half_dim = HEAD_DIM // 2
    turned = jnp.concatenate([-values[..., half_dim:], values[..., :half_dim]], axis=-1)
    return values * cosine[:, None, :] + turned * sine[:, None, :]


def unrotate(grads_in, cosine, sine):
    half_dim = HEAD_DIM // 2
    shifted = grads_in * sine[:, None, :]
    turned = jnp.concatenate([shifted[..., half_dim:], -shifted[..., :half_dim]], axis=-1)
    return grads_in * cosine[:, None, :] + turned


def row_stats(values):
    summed = lax.psum(jnp.sum(values, axis=-1), "tensor")
    center = summed / D
    centered = values - center[..., None]
    spread = lax.psum(jnp.sum(centered * centered, axis=-1), "tensor") / D
    inverse = lax.rsqrt(spread + EPSILON)[..., None]
    return (centered * inverse, inverse)


def norm_back(incoming, normed, inverse, gain):
    scaled = incoming * gain
    left_sum, right_sum = lax.psum(
        (jnp.sum(scaled, axis=-1), jnp.sum(scaled * normed, axis=-1)), "tensor"
    )
    result = inverse * (scaled - left_sum[..., None] / D - normed * right_sum[..., None] / D)
    return (result, jnp.sum(incoming * normed, axis=(0, 1)))


def feature_rows(values):
    return lax.all_gather(values, "tensor", axis=2, tiled=True)


def feature_sums(values):
    return lax.psum_scatter(values, "tensor", scatter_dimension=2, tiled=True)


def attend_head(triple):
    queries, keys_all, values_all = triple
    scores = jnp.dot(queries, keys_all.T, precision=EXACT_PRECISION) * HEAD_DIM ** (-0.5)
    largest = jnp.max(scores, axis=-1, keepdims=True)
    weights = jnp.exp(scores - largest)
    summed = jnp.sum(weights, axis=-1, keepdims=True)
    log_total = largest[:, 0] + jnp.log(summed[:, 0])
    attended = jnp.dot(weights, values_all, precision=EXACT_PRECISION) / summed
    return (attended, log_total)


def head_back(operands):
    queries, keys_all, values_all, grad_attended, attended, log_total = operands
    scores = jnp.dot(queries, keys_all.T, precision=EXACT_PRECISION) * HEAD_DIM ** (-0.5)
    weights = jnp.exp(scores - log_total[:, None])
    value_part = jnp.dot(weights.T, grad_attended, precision=EXACT_PRECISION)
    grad_weights = jnp.dot(grad_attended, values_all.T, precision=EXACT_PRECISION)
    delta = jnp.sum(grad_attended * attended, axis=-1)
    grad_scores = weights * (grad_weights - delta[:, None]) * HEAD_DIM ** (-0.5)
    grad_queries = jnp.dot(grad_scores, keys_all, precision=EXACT_PRECISION)
    key_part = jnp.dot(grad_scores.T, queries, precision=EXACT_PRECISION)
    return (grad_queries, key_part, value_part)


def query_blocks(values, rows):
    count = values.shape[0] // rows
    return jnp.transpose(
        values.reshape(count, rows, values.shape[1], values.shape[2]), (0, 2, 1, 3)
    )


def attend_sequence(triple):
    queries, keys_all, values_all = triple
    block_rows = queries.shape[0]
    rows = min(512, block_rows)
    keys_heads = jnp.transpose(keys_all, (1, 0, 2))
    values_heads = jnp.transpose(values_all, (1, 0, 2))

    def one_block(query_heads):
        return lax.map(attend_head, (query_heads, keys_heads, values_heads))

    attended, log_total = lax.map(one_block, query_blocks(queries, rows))
    attended = jnp.transpose(attended, (0, 2, 1, 3)).reshape(queries.shape)
    return (attended, log_total)


def attend_sequence_back(operands):
    queries, keys_all, values_all, grad_attended, attended, log_total = operands
    block_rows = queries.shape[0]
    rows = min(512, block_rows)
    keys_heads = jnp.transpose(keys_all, (1, 0, 2))
    values_heads = jnp.transpose(values_all, (1, 0, 2))

    def one_block(totals, pieces):
        query_heads, grad_heads, attended_heads, log_heads = pieces
        grad_queries, key_part, value_part = lax.map(
            head_back,
            (query_heads, keys_heads, values_heads, grad_heads, attended_heads, log_heads),
        )
        return ((totals[0] + key_part, totals[1] + value_part), grad_queries)

    empty = jnp.zeros(keys_heads.shape, jnp.float32)
    totals, grad_queries = lax.scan(
        one_block,
        (empty, empty),
        (
            query_blocks(queries, rows),
            query_blocks(grad_attended, rows),
            query_blocks(attended, rows),
            log_total,
        ),
    )
    grad_queries = jnp.transpose(grad_queries, (0, 2, 1, 3)).reshape(queries.shape)
    return (grad_queries, jnp.transpose(totals[0], (1, 0, 2)), jnp.transpose(totals[1], (1, 0, 2)))


def body(
    inputs,
    out_grad,
    attn_gain,
    query_key_value_weight,
    attention_output_weight,
    mlp_gain,
    feedforward_input_weight,
    feedforward_output_weight,
):
    seq_count, block_rows, local_width = inputs.shape
    head_cols = query_key_value_weight.shape[2]
    local_heads = head_cols // HEAD_DIM
    positions = (
        lax.axis_index("ctx") * block_rows + jnp.arange(block_rows, dtype=jnp.int32)
    ).astype(jnp.float32)
    cosine, sine = rope_tables(positions)
    head_shape = (seq_count, block_rows, local_heads, HEAD_DIM)
    normed_one, inverse_one = row_stats(inputs)
    hidden_one = feature_rows(normed_one * attn_gain)
    projected_rows = jnp.einsum(
        "sbd,dtc->sbtc", hidden_one, query_key_value_weight, precision=EXACT_PRECISION
    )
    queries = rotate(projected_rows[:, :, 0].reshape(head_shape), cosine, sine)
    keys_flat = rotate(projected_rows[:, :, 1].reshape(head_shape), cosine, sine).reshape(
        seq_count, block_rows, head_cols
    )
    values_flat = projected_rows[:, :, 2]
    all_keys, all_values = (
        lax.all_gather(keys_flat, "ctx", axis=1, tiled=True),
        lax.all_gather(values_flat, "ctx", axis=1, tiled=True),
    )
    seq_len = all_keys.shape[1]
    full_shape = (seq_count, seq_len, local_heads, HEAD_DIM)
    attended, log_total = lax.map(
        attend_sequence, (queries, all_keys.reshape(full_shape), all_values.reshape(full_shape))
    )
    flattened_heads = attended.reshape(seq_count, block_rows, head_cols)
    residual_stream = inputs + feature_sums(
        jnp.einsum(
            "sbc,cd->sbd", flattened_heads, attention_output_weight, precision=EXACT_PRECISION
        )
    )
    normed_two, inverse_two = row_stats(residual_stream)
    second_hidden = feature_rows(normed_two * mlp_gain)
    widened_hidden = jnp.einsum(
        "sbd,dtf->sbtf", second_hidden, feedforward_input_weight, precision=EXACT_PRECISION
    )
    activated, gelu_pull = jax.vjp(
        lambda inner: jax.nn.gelu(inner, approximate=False), widened_hidden[:, :, 0]
    )
    gated_product = activated * widened_hidden[:, :, 1]
    layer_out = residual_stream + feature_sums(
        jnp.einsum(
            "sbf,fd->sbd", gated_product, feedforward_output_weight, precision=EXACT_PRECISION
        )
    )
    grad_full = feature_rows(out_grad)
    out_weight_grad = jnp.einsum("sbf,sbd->fd", gated_product, grad_full, precision=EXACT_PRECISION)
    grad_product = jnp.einsum(
        "sbd,fd->sbf", grad_full, feedforward_output_weight, precision=EXACT_PRECISION
    )
    grad_active = gelu_pull(grad_product * widened_hidden[:, :, 1])[0]
    grad_expanded = jnp.stack([grad_active, grad_product * activated], axis=2)
    in_weight_grad = jnp.einsum(
        "sbd,sbtf->dtf", second_hidden, grad_expanded, precision=EXACT_PRECISION
    )
    grad_hidden_two = feature_sums(
        jnp.einsum(
            "sbtf,dtf->sbd", grad_expanded, feedforward_input_weight, precision=EXACT_PRECISION
        )
    )
    grad_norm_two, gain_two_grad = norm_back(grad_hidden_two, normed_two, inverse_two, mlp_gain)
    grad_residual = out_grad + grad_norm_two
    mlp_totals = (out_weight_grad, in_weight_grad, gain_two_grad)
    grad_branch = feature_rows(grad_residual)
    attn_weight_grad = jnp.einsum(
        "sbc,sbd->cd", flattened_heads, grad_branch, precision=EXACT_PRECISION
    )
    grad_heads = jnp.einsum(
        "sbd,cd->sbc", grad_branch, attention_output_weight, precision=EXACT_PRECISION
    ).reshape(head_shape)
    back_keys, back_values = (all_keys, all_values)
    grad_queries, key_part, value_part = lax.map(
        attend_sequence_back,
        (
            queries,
            back_keys.reshape(full_shape),
            back_values.reshape(full_shape),
            grad_heads,
            attended,
            log_total,
        ),
    )
    key_grad, value_grad = (
        lax.psum_scatter(
            key_part.reshape(seq_count, seq_len, head_cols), "ctx", scatter_dimension=1, tiled=True
        ),
        lax.psum_scatter(
            value_part.reshape(seq_count, seq_len, head_cols),
            "ctx",
            scatter_dimension=1,
            tiled=True,
        ),
    )
    grad_q = unrotate(grad_queries, cosine, sine).reshape(seq_count, block_rows, head_cols)
    grad_k = unrotate(key_grad.reshape(head_shape), cosine, sine).reshape(
        seq_count, block_rows, head_cols
    )
    grad_joint = jnp.stack([grad_q, grad_k, value_grad], axis=2)
    qkv_weight_grad = jnp.einsum("sbd,sbtc->dtc", hidden_one, grad_joint, precision=EXACT_PRECISION)
    grad_hidden_one = feature_sums(
        jnp.einsum("sbtc,dtc->sbd", grad_joint, query_key_value_weight, precision=EXACT_PRECISION)
    )
    grad_norm_one, gain_one_grad = norm_back(grad_hidden_one, normed_one, inverse_one, attn_gain)
    input_grad = grad_residual + grad_norm_one
    gain_one_total, qkv_total, attn_total, gain_two_total, in_total, out_total = lax.psum(
        (
            gain_one_grad,
            qkv_weight_grad,
            attn_weight_grad,
            mlp_totals[2],
            mlp_totals[1],
            mlp_totals[0],
        ),
        ("dp", "ctx"),
    )
    return (
        layer_out,
        input_grad,
        gain_one_total,
        qkv_total,
        attn_total,
        gain_two_total,
        in_total,
        out_total,
    )


def solution(mesh):
    in_specs = (
        P("dp", "ctx", "tensor"),
        P("dp", "ctx", "tensor"),
        P("tensor"),
        P(None, None, "tensor"),
        P("tensor", None),
        P("tensor"),
        P(None, None, "tensor"),
        P("tensor", None),
    )
    out_specs = (
        P("dp", "ctx", "tensor"),
        P("dp", "ctx", "tensor"),
        P("tensor"),
        P(None, None, "tensor"),
        P("tensor", None),
        P("tensor"),
        P(None, None, "tensor"),
        P("tensor", None),
    )
    return jax.shard_map(body, mesh=mesh, in_specs=in_specs, out_specs=out_specs, check_vma=False)
```

profile of v0, /device:TPU:0, one launch (start us, length us, event | category | flops | bytes accessed | tf_op | source)
XLA Modules:
  0.0 1947.9 jit_solution(17698572751524802824)
XLA Ops:
  19.5 14.8 all-gather.8.cloned.1.call-done
  34.3 14.3 fusion.153
  80.8 88.3 %all-gather.18.cloned.1.call-done = f32[1,4096,1,384]{1,3,2,0:T(8,128)} async-done(((f32[1,1024,1,384]{1,3,2,0:T(8,128)}), f32[1,4096,1,384]{1,3,2,0:T(8,128)}) %all-gather.18.cloned.1.call-update) | async-done | bytes 6291472 | tf_op jit(solution)/shard_map/all_gather | solution.py:169
  178.8 106.1 %all-gather.10.cloned.1.call-done = f32[1,4096,384]{1,2,0:T(8,128)} async-done(((f32[1,1024,384]{1,2,0:T(8,128)}), f32[1,4096,384]{1,2,0:T(8,128)}) %all-gather.10.cloned.1.call-update) | async-done | bytes 6291472 | tf_op jit(solution)/shard_map/all_gather | solution.py:168
  295.8 292.6 %while.81 = (s32[]{:T(128)}, f32[2,6,512,64]{2,3,1,0:T(8,128)}, f32[2,6,512]{2,1,0:T(8,128)}, f32[2,6,512,64]{3,2,1,0:T(8,128)}, f32[6,4096,64]{2,1,0:T(8,128)},...) while((s32[]{:T(128)}, f32[2,6,512,64]{2,3,1,0:T(8,128)}, f32[2,6,512]{2,1,0:T(8,128)}, ...), condition=%wide.region_9.10_spmd.clone, body=%wide.region_4.9_spmd.sunk.clone | while | flops 3235937792 | bytes 32954640 | solution.py:104
  298.7 139.9 %while.80 = (s32[]{:T(128)}, f32[6,512,64]{1,2,0:T(8,128)}, f32[6,512]{1,0:T(8,128)}, f32[6,512,64]{2,1,0:T(8,128)}, f32[6,4096,64]{2,1,0:T(8,128)}, /*index=5*/f32[6,4096,64]{2,1,0:T(8,128)}, s32[]{:T(128)}, s32[]{:T(128)}) while((s32[]{:T(128)}, f32[6,512,64]{1,2,0:T(8,128)}, f32[6,512]{1,0:T(8,128)}, f32[6,512,64]{2,1,0:T(8,128)}, ...), condition=%wide.region_8.8_spmd, body=%wide.region_5.7_spmd.sunk | while | flops 3235937792 | bytes 29775968 | solution.py:102
  309.1 11.5 fusion.286
  332.4 11.5 fusion.286
  355.7 11.5 fusion.286
  379.1 11.5 fusion.286
  402.4 11.5 fusion.286
  425.7 11.5 fusion.286
  444.6 139.9 %while.80 = (s32[]{:T(128)}, f32[6,512,64]{1,2,0:T(8,128)}, f32[6,512]{1,0:T(8,128)}, f32[6,512,64]{2,1,0:T(8,128)}, f32[6,4096,64]{2,1,0:T(8,128)}, /*index=5*/f32[6,4096,64]{2,1,0:T(8,128)}, s32[]{:T(128)}, s32[]{:T(128)}) while((s32[]{:T(128)}, f32[6,512,64]{1,2,0:T(8,128)}, f32[6,512]{1,0:T(8,128)}, f32[6,512,64]{2,1,0:T(8,128)}, ...), condition=%wide.region_8.8_spmd, body=%wide.region_5.7_spmd.sunk | while | flops 3235937792 | bytes 29775968 | solution.py:102
  455.1 11.5 fusion.286
  478.4 11.5 fusion.286
  501.7 11.5 fusion.286
  525.0 11.5 fusion.286
  548.4 11.5 fusion.286
  571.7 11.5 fusion.286
  639.1 13.4 fusion.156
  661.8 14.8 fusion.163
  678.2 11.7 fusion.161
  706.7 13.4 all-gather.16.cloned.1.call-done
  728.4 604.8 %while.83 = (s32[]{:T(128)}, f32[6,4096,64]{1,2,0:T(8,128)}, f32[6,4096,64]{1,2,0:T(8,128)}, f32[2,6,512,64]{2,3,1,0:T(8,128)}, f32[2,6,512,64]{3,2,1,0:T(8,128)...) while((s32[]{:T(128)}, f32[6,4096,64]{1,2,0:T(8,128)}, ...), condition=%wide.region_25.26_spmd.clone.clone, body=%wide.region_21.25_spmd.clone.sunk.clone | while | flops 8074100224 | bytes 123119064 | solution.py:125
  757.4 268.5 %while.82 = (s32[]{:T(128)}, f32[6,512,64]{1,2,0:T(8,128)}, f32[6,4096,64]{1,2,0:T(8,128)}, f32[6,4096,64]{1,2,0:T(8,128)}, f32[6,512,64]{2,1,0:T(8,128)S(1)}, /...) while((s32[]{:T(128)}, f32[6,512,64]{1,2,0:T(8,128)}, ...), condition=%wide.region_24.24_spmd, body=%wide.region_22.23_spmd.sunk | while | flops 8067808768 | bytes 60179580 | solution.py:118
  785.1 10.6 fusion.281
  829.9 10.6 fusion.281
  864.3 10.3 multiply_multiply_fusion.7
  874.6 10.6 fusion.281
  919.4 10.6 fusion.281
  964.1 10.6 fusion.281
  1008.8 10.6 fusion.281
  1042.4 268.5 %while.82 = (s32[]{:T(128)}, f32[6,512,64]{1,2,0:T(8,128)}, f32[6,4096,64]{1,2,0:T(8,128)}, f32[6,4096,64]{1,2,0:T(8,128)}, f32[6,512,64]{2,1,0:T(8,128)S(1)}, /...) while((s32[]{:T(128)}, f32[6,512,64]{1,2,0:T(8,128)}, ...), condition=%wide.region_24.24_spmd, body=%wide.region_22.23_spmd.sunk | while | flops 8067808768 | bytes 60179580 | solution.py:118
  1070.1 10.6 fusion.281
  1114.8 10.6 fusion.281
  1159.6 10.6 fusion.281
  1204.3 10.6 fusion.281
  1249.0 10.6 fusion.281
  1293.8 10.6 fusion.281
  1310.9 14.9 select_add_fusion.4
  1356.0 95.9 %reduce-scatter.13.cloned.1.call-done = f32[1,1024,384]{2,1,0:T(8,128)} async-done(((f32[1,4096,384]{2,1,0:T(8,128)}), f32[1,1024,384]{2,1,0:T(8,128)}) %reduce-scatter.13.cloned.1.call-update) | async-done | bytes 1572880 | tf_op jit(solution)/shard_map/reduce_scatter | solution.py:234
  1465.7 99.9 %reduce-scatter.15.cloned.1.call-done = f32[1,1024,384]{2,1,0:T(8,128)} async-done(((f32[1,4096,384]{2,1,0:T(8,128)}), f32[1,1024,384]{2,1,0:T(8,128)}) %reduce-scatter.15.cloned.1.call-update) | async-done | bytes 1572880 | tf_op jit(solution)/shard_map/reduce_scatter | solution.py:237
  1565.6 16.9 fusion.162
  1584.3 15.3 fusion.58
  1599.6 14.3 fusion.64
  1619.1 14.7 fusion.60
  1637.3 44.3 %all-reduce = (f32[384]{0:T(512)}, f32[384]{0:T(512)}) all-reduce(f32[384]{0:T(512)S(1)} %get-tuple-element.299, f32[384]{0:T(512)S(1)} %copy-done.44), channel_id=1, replica_groups=mesh['dp'=4,'ctx'=4,'tensor'=2] {'dp','ctx'}, use_global_device_ids=true, to_apply=%region_34.35 | all-reduce | flops 768 | bytes 6144 | tf_op jit(solution)/shard_map/psum | solution.py:255
  1687.0 244.9 %all-reduce.6.cloned.1.call-done = (f32[768,3,384]{2,0,1:T(8,128)}, f32[384,768]{1,0:T(8,128)}, f32[768,2,576]{0,2,1:T(8,128)}, f32[576,768]{1,0:T(8,128)}) async-done(((f32[768,3,384]{2,0,1:T(8,128)}, f32[384,768]{1,0:T(8,128)}, f32[768,2,576]{0,2,1:T(8,128)}, f32[576,768]{1,0:T(8,128)}), (f32[768,3,384]{2,0,1:T(8,128)}, f32[384,768]{1,0:T(8,128)}, f32[768,2,576]{0,2,1:T(8,128)}, ...) | async-done | bytes 10027024 | tf_op jit(solution)/shard_map/psum | solution.py:255
  (357 shorter events, 789.8 us)
Async XLA Ops:
  7.2 631.9 %copy-start = (f32[768,2,576]{0,2,1:T(8,128)S(1)}, f32[768,2,576]{0,2,1:T(8,128)}, u32[]{:S(2)}) copy-start(f32[768,2,576]{0,2,1:T(8,128)} %param.22) | copy-start | bytes 10616836
  7.2 9.3 copy-start.41
  7.2 27.1 %all-gather.8.cloned.1.call-start = ((), (), s32[]{:S(2)}) async-start(), calls=%async_computation.6 | async-start | bytes 4718592 | tf_op jit(solution)/shard_map/all_gather | solution.py:56
  11.6 7.8 copy-start.37
  19.4 149.7 %all-gather.18.cloned.1.call-start = ((), (), s32[]{:S(2)}) async-start(), calls=%async_computation.17 | async-start | bytes 7864320 | tf_op jit(solution)/shard_map/all_gather | solution.py:169
  48.6 3.8 copy-start.13
  52.4 232.4 %all-gather.10.cloned.1.call-start = ((), (), s32[]{:S(2)}) async-start(), calls=%async_computation.7 | async-start | bytes 7864320 | tf_op jit(solution)/shard_map/all_gather | solution.py:168
  53.3 1.9 copy-start.25
  53.3 1.9 copy-start.27
  58.3 550.7 %reduce-scatter.7.cloned.1.call-start = ((), (), s32[]{:S(2)}) async-start(), calls=%async_computation.8 | async-start | bytes 4718592 | tf_op jit(solution)/shard_map/reduce_scatter | solution.py:60
  599.7 24.0 %all-gather.14.cloned.1.call-start = ((), (), s32[]{:S(2)}) async-start(), calls=%async_computation.11 | async-start | bytes 4718592 | tf_op jit(solution)/shard_map/all_gather | solution.py:56
  600.3 18.6 copy-start.43
  600.3 38.8 %all-gather.12.cloned.1.call-start = ((), (), s32[]{:S(2)}) async-start(), calls=%async_computation.9 | async-start | bytes 4718592 | tf_op jit(solution)/shard_map/all_gather | solution.py:56
  622.0 68.0 %reduce-scatter.11.cloned.1.call-start = ((), (), s32[]{:S(2)}) async-start(), calls=%async_computation.12 | async-start | bytes 4718592 | tf_op jit(solution)/shard_map/reduce_scatter | solution.py:60
  639.1 13.4 copy-start.5
  652.5 6.0 copy-start.3
  658.5 2.2 copy-start.29
  676.6 26.5 %reduce-scatter.9.cloned.1.call-start = ((), (), s32[]{:S(2)}) async-start(), calls=%async_computation.10 | async-start | bytes 4718592 | tf_op jit(solution)/shard_map/reduce_scatter | solution.py:60
  689.9 13.2 copy-start.20
  690.0 30.1 %all-gather.16.cloned.1.call-start = ((), (), s32[]{:S(2)}) async-start(), calls=%async_computation.13 | async-start | bytes 4718592 | tf_op jit(solution)/shard_map/all_gather | solution.py:56
  706.6 13.5 copy-start.15
  706.6 745.2 %reduce-scatter.13.cloned.1.call-start = ((), (), s32[]{:S(2)}) async-start(), calls=%async_computation.14 | async-start | bytes 7864320 | tf_op jit(solution)/shard_map/reduce_scatter | solution.py:234
  720.1 8.3 copy-start.36
  1025.9 9.1 copy-start.8
  1025.9 9.1 copy-start.16
  1310.9 14.9 copy-start.8
  1310.9 14.9 copy-start.16
  1339.8 225.8 %reduce-scatter.15.cloned.1.call-start = ((), (), s32[]{:S(2)}) async-start(), calls=%async_computation.15 | async-start | bytes 7864320 | tf_op jit(solution)/shard_map/reduce_scatter | solution.py:237
  1346.5 2.8 copy-start.18
  1346.5 287.3 %reduce-scatter.17.cloned.1.call-start = ((), (), s32[]{:S(2)}) async-start(), calls=%async_computation.16 | async-start | bytes 4718592 | tf_op jit(solution)/shard_map/reduce_scatter | solution.py:60
  1355.9 98.9 %copy-start.19 = (f32[1,1024,6,64]{1,3,2,0:T(8,128)S(1)}, f32[1,1024,6,64]{1,3,2,0:T(8,128)}, u32[]{:S(2)}) copy-start(f32[1,1024,6,64]{1,3,2,0:T(8,128)} %broadcast_in_dim.64) | copy-start | bytes 4718596
  1356.0 98.9 %copy-start.26 = (f32[1024,64]{0,1:T(8,128)S(1)}, f32[1024,64]{0,1:T(8,128)}, u32[]{:S(2)}) copy-start(f32[1024,64]{0,1:T(8,128)} %copy-done.25) | copy-start | bytes 786436
  1465.7 99.9 %copy-start.32 = (f32[1,1024,1,384]{3,1,2,0:T(8,128)}, f32[1,1024,1,384]{3,1,2,0:T(8,128)S(1)}, u32[]{:S(2)}) copy-start(f32[1,1024,1,384]{3,1,2,0:T(8,128)S(1)} %get-tuple-element.388) | copy-start | bytes 4718596
  1582.5 1.9 copy-start.24
  1582.5 349.4 %all-reduce.6.cloned.1.call-start = ((), (), s32[]{:S(2)}) async-start(), calls=%async_computation.18 | async-start | bytes 20054016 | tf_op jit(solution)/shard_map/psum | solution.py:255
  1584.3 15.3 copy-start.23
  1599.6 14.3 copy-start.10
  1599.6 14.3 copy-start.12
  1599.6 19.4 copy-start.45
  1613.9 5.1 copy-start.33
  1613.9 5.1 copy-start.34
  1613.9 5.1 copy-start.46
  1633.8 3.5 copy-start.44
  1633.8 50.3 %copy-start.11 = (f32[1,1024,384]{2,1,0:T(8,128)S(1)}, f32[1,1024,384]{2,1,0:T(8,128)}, u32[]{:S(2)}) copy-start(f32[1,1024,384]{2,1,0:T(8,128)} %get-tuple-element.394) | copy-start | bytes 4718596
  1931.9 4.2 copy-start.35
  1931.9 5.2 copy-start.22
  1937.1 2.8 copy-start.31
  1937.1 4.0 copy-start.1
  (15 other events, 20.2 us)
Sparse Core Ops, SparseCore 0:
  19.5 14.6 all-gather.7
  52.6 116.5 all-gather.17
  171.3 113.5 all-gather.9
  599.8 9.0 reduce-scatter.6
  610.4 13.2 all-gather.13
  625.8 13.2 all-gather.11
  676.7 12.0 reduce-scatter.10
  691.0 12.0 reduce-scatter.8
  706.7 13.2 all-gather.15
  1339.9 111.9 reduce-scatter.12
  1454.3 111.2 reduce-scatter.14
  1582.6 11.4 reduce-scatter.16
  1633.9 297.9 all-reduce.5
where the time goes:
time: 1960 us; the launch traced here: 1950 us
  matrix products  912 us (47%)
  waiting for transfers between devices  687 us (35%)
  local copies, waits for them, and re-layouts  133 us (7%)
  other arithmetic  110 us (6%)
  blocking collectives  59.2 us (3%)
  loops' own time  30.3 us (2%)
    psum x1, waiting for transfers between devices, body(): lax.psum((gain_one_grad, qkv_weight_grad, attn_weight_grad, mlp_totals[2]...  245 us
    dot_general x12, matrix products, attend_head(): attended = jnp.dot(weights, values_all, precision=EXACT_PRECISION) / summed  138 us
    dot_general x12, matrix products, head_back(): grad_queries = jnp.dot(grad_scores, keys_all, precision=EXACT_PRECISION)  127 us
    dot_general x12, matrix products, head_back(): jnp.dot(grad_attended, values_all.T, precision=EXACT_PRECISION)  124 us
    dot_general x12, matrix products, attend_head(): jnp.dot(queries, keys_all.T, precision=EXACT_PRECISION) * HEAD_DIM ** (-0.5)  107 us
    all_gather x1, waiting for transfers between devices, body(): lax.all_gather(keys_flat, 'ctx', axis=1, tiled=True)  106 us
    dot_general x12, matrix products, head_back(): jnp.dot(queries, keys_all.T, precision=EXACT_PRECISION) * HEAD_DIM ** (-0.5)  103 us
    reduce_scatter x1, waiting for transfers between devices, body(): lax.psum_scatter(value_part.reshape(seq_count, seq_len, head_cols), 'ctx'...  99.9 us
  transfers between devices with their start and end apart: 13, of which 11 were waited for; matrix products, arithmetic and copies ran while one was open for 8% of the time, Pallas kernels for 0%

commit v1 on v0

v1 whole, which is shorter than its diff:
```python
import functools
import math

import jax
import jax.numpy as jnp
from jax import lax
from jax.experimental import pallas as pl
from jax.experimental.pallas import tpu as pltpu
from jax.sharding import PartitionSpec as P

HEAD_DIM = 64
PAIR = 2 * HEAD_DIM
EPSILON = 1e-05
ROPE_BASE = 160000.0
PRECISION = lax.Precision.HIGH
CHUNKS = 2
VMEM = 56 * 1024 * 1024
LOG2E = math.log2(math.e)
NT = (((1,), (1,)), ((), ()))
TN = (((0,), (0,)), ((), ()))


def rope_tables(positions):
    half_dim = HEAD_DIM // 2
    frequency = jnp.power(ROPE_BASE, -2.0 * jnp.arange(half_dim, dtype=jnp.float32) / HEAD_DIM)
    angles = positions[:, None] * frequency[None, :]
    return jnp.tile(jnp.cos(angles), (1, 4)), jnp.tile(jnp.sin(angles), (1, 4))


def first_half(shape):
    return lax.rem(lax.broadcasted_iota(jnp.int32, shape, 1), HEAD_DIM) < HEAD_DIM // 2


def split(values):
    high = values.astype(jnp.bfloat16)
    low = (values - high.astype(jnp.float32)).astype(jnp.bfloat16)
    return high, low


def pack_kernel(rotary, scale, order, x_ref, cos_ref, sin_ref, out_ref):
    x = x_ref[...]
    if rotary:
        quarter = HEAD_DIM // 2
        turned = jnp.where(
            first_half(x.shape), -pltpu.roll(x, PAIR - quarter, 1), pltpu.roll(x, quarter, 1)
        )
        x = x * cos_ref[...] + turned * sin_ref[...]
    if scale != 1.0:
        x = x * scale
    parts = split(x)
    for head in range(2):
        pieces = [part[:, head * HEAD_DIM : (head + 1) * HEAD_DIM] for part in parts]
        out_ref[:, head * 256 : (head + 1) * 256] = jnp.concatenate(
            [pieces[index] for index in order], axis=1
        )


def pack(x, cosine, sine, rotary, scale, order):
    rows, cols = x.shape
    block = min(512, rows)
    table = pl.BlockSpec((block, PAIR), lambda i, j: (i, 0))
    return pl.pallas_call(
        functools.partial(pack_kernel, rotary, scale, order),
        grid=(rows // block, cols // PAIR),
        in_specs=[pl.BlockSpec((block, PAIR), lambda i, j: (i, j)), table, table],
        out_specs=pl.BlockSpec((block, 512), lambda i, j: (i, j)),
        out_shape=jax.ShapeDtypeStruct((rows, cols * 4), jnp.bfloat16),
        compiler_params=pltpu.CompilerParams(vmem_limit_bytes=VMEM),
        cost_estimate=pl.CostEstimate(
            flops=rows * cols * 8, bytes_accessed=rows * cols * 12, transcendentals=0
        ),
    )(x, cosine, sine)


LEFT = (0, 1, 0, 1)
RIGHT = (0, 1, 1, 0)


def dot(a, b, dims=(((1,), (0,)), ((), ()))):
    return lax.dot_general(a, b, dims, preferred_element_type=jnp.float32)


def attend_kernel(step, q_ref, k_ref, v_ref, o_ref, lse_ref):
    rows = q_ref.shape[0]
    outs, logs = [], []
    for head in range(2):
        at = head * 256
        q = q_ref[:, at : at + 256]
        most = jnp.full((rows, 1), -jnp.inf, jnp.float32)
        total = jnp.zeros((rows, 1), jnp.float32)
        acc = jnp.zeros((rows, PAIR), jnp.float32)
        for start in range(0, k_ref.shape[0], step):
            s = dot(q, k_ref[start : start + step, at : at + 256], NT)
            new = jnp.maximum(most, jnp.max(s, axis=1, keepdims=True))
            p = jnp.exp2(s - new)
            shrink = jnp.exp2(most - new)
            total = total * shrink + jnp.sum(p, axis=1, keepdims=True)
            high, low = split(p)
            v = v_ref[start : start + step, at : at + PAIR]
            acc = acc * shrink + (dot(high, v) + dot(low, v))
            most = new
        outs.append((acc[:, :HEAD_DIM] + acc[:, HEAD_DIM:]) / total)
        logs.append(jnp.broadcast_to(most + jnp.log2(total), (rows, HEAD_DIM)))
    o_ref[...] = jnp.concatenate(outs, axis=1)
    lse_ref[...] = jnp.concatenate(logs, axis=1)


def attend(q, k, v):
    rows, cols = q.shape
    keys = k.shape[0]
    block = min(256, rows)
    pairs = cols // 512
    wide = pl.BlockSpec((keys, 512), lambda i, j: (0, i))
    narrow = pl.BlockSpec((block, PAIR), lambda i, j: (j, i))
    shape = jax.ShapeDtypeStruct((rows, pairs * PAIR), jnp.float32)
    return pl.pallas_call(
        functools.partial(attend_kernel, min(1024, keys)),
        grid=(pairs, rows // block),
        in_specs=[pl.BlockSpec((block, 512), lambda i, j: (j, i)), wide, wide],
        out_specs=[narrow, narrow],
        out_shape=[shape, shape],
        compiler_params=pltpu.CompilerParams(vmem_limit_bytes=VMEM),
        cost_estimate=pl.CostEstimate(
            flops=2 * rows * keys * pairs * 2 * 256 * 3,
            bytes_accessed=(rows + keys) * cols * 4,
            transcendentals=rows * keys * pairs * 2,
        ),
    )(q, k, v)


def attend_back_kernel(
    step, q_ref, do_ref, k_ref, v_ref, stat_ref, cos_ref, sin_ref, dk_ref, dv_ref, dq_ref
):
    @pl.when(pl.program_id(1) == 0)
    def _():
        dq_ref[...] = jnp.zeros_like(dq_ref)

    keys = k_ref.shape[0]
    dks, dvs = [], []
    for head in range(2):
        at = head * 256
        k = k_ref[:, at : at + 256]
        v = v_ref[:, at : at + 256]
        k_turned = k_ref[:, at : at + PAIR].astype(jnp.float32).T.astype(jnp.bfloat16)
        dk = jnp.zeros((keys, PAIR), jnp.float32)
        dv = jnp.zeros((keys, PAIR), jnp.float32)
        for start in range(0, q_ref.shape[0], step):
            q = q_ref[start : start + step, at : at + 256]
            do = do_ref[start : start + step, at : at + 256]
            lse = stat_ref[0, head : head + 1, start : start + step]
            delta = stat_ref[0, 2 + head : 3 + head, start : start + step]
            p = jnp.exp2(dot(k, q, NT) - lse)
            ds = p * (dot(v, do, NT) - delta)
            p_high, p_low = split(p)
            dv = dv + (dot(p_high, do[:, :PAIR]) + dot(p_low, do[:, :PAIR]))
            ds_high, ds_low = split(ds)
            dk = dk + (dot(ds_high, q[:, :PAIR]) + dot(ds_low, q[:, :PAIR]))
            dq = dot(k_turned, ds_high) + dot(k_turned, ds_low)
            dq_ref[head * HEAD_DIM : (head + 1) * HEAD_DIM, start : start + step] += (
                dq[:HEAD_DIM] + dq[HEAD_DIM:]
            )
        dks.append(dk[:, :HEAD_DIM] + dk[:, HEAD_DIM:])
        dvs.append(dv[:, :HEAD_DIM] + dv[:, HEAD_DIM:])
    dk = jnp.concatenate(dks, axis=1) * (1.0 / LOG2E)
    shifted = dk * sin_ref[...]
    quarter = HEAD_DIM // 2
    turned = jnp.where(
        first_half(dk.shape),
        pltpu.roll(shifted, PAIR - quarter, 1),
        -pltpu.roll(shifted, quarter, 1),
    )
    dk_ref[...] = dk * cos_ref[...] + turned
    dv_ref[...] = jnp.concatenate(dvs, axis=1)


def attend_back(q, do, k, v, stats, cosine, sine):
    rows, cols = q.shape
    keys = k.shape[0]
    block = min(512, keys)
    pairs = cols // 512
    whole = pl.BlockSpec((rows, 512), lambda i, j: (0, i))
    tile = pl.BlockSpec((block, 512), lambda i, j: (j, i))
    table = pl.BlockSpec((block, PAIR), lambda i, j: (j, 0))
    narrow = pl.BlockSpec((block, PAIR), lambda i, j: (j, i))
    shape = jax.ShapeDtypeStruct((keys, pairs * PAIR), jnp.float32)
    return pl.pallas_call(
        functools.partial(attend_back_kernel, min(512, rows)),
        grid=(pairs, keys // block),
        in_specs=[
            whole,
            whole,
            tile,
            tile,
            pl.BlockSpec((1, 8, rows), lambda i, j: (i, 0, 0)),
            table,
            table,
        ],
        out_specs=[narrow, narrow, pl.BlockSpec((PAIR, rows), lambda i, j: (i, 0))],
        out_shape=[shape, shape, jax.ShapeDtypeStruct((pairs * PAIR, rows), jnp.float32)],
        compiler_params=pltpu.CompilerParams(vmem_limit_bytes=VMEM),
        cost_estimate=pl.CostEstimate(
            flops=2 * rows * keys * pairs * 2 * 256 * 8,
            bytes_accessed=(rows + keys) * cols * 4,
            transcendentals=rows * keys * pairs * 2,
        ),
    )(q, do, k, v, stats, cosine, sine)


def normalize(values):
    centered = values - jnp.mean(values, axis=-1, keepdims=True)
    inverse = lax.rsqrt(jnp.mean(centered * centered, axis=-1, keepdims=True) + EPSILON)
    return centered * inverse, inverse


def matmul(spec, left, right):
    return jnp.einsum(spec, left, right, precision=PRECISION)


def body(inputs, out_grad, attn_gain, qkv_weight, attn_out_weight, mlp_gain, ff_in, ff_out):
    x_half, c_half = inputs[0], out_grad[0]
    rows, half = x_half.shape
    ctx_count = lax.axis_size("ctx")
    tensor_index = lax.axis_index("tensor")
    piece = rows // CHUNKS
    first = lax.axis_index("ctx") * rows

    def own_features(values):
        return lax.dynamic_slice_in_dim(values, tensor_index * half, half, values.ndim - 1)

    def features(values):
        return lax.all_gather(values, "tensor", axis=values.ndim - 1, tiled=True)

    gain_one, gain_two = features(attn_gain), features(mlp_gain)

    x_own = features(x_half)
    far, gathered = None, []
    for index in range(CHUNKS):
        part = x_half[index * piece : (index + 1) * piece]
        if far is not None:
            part, _ = lax.optimization_barrier((part, far))
        far = lax.all_gather(part, "ctx", axis=0, tiled=True)
        gathered.append(far)

    normed_one, inverse_one = normalize(x_own)
    hidden_own = normed_one * gain_one
    own_cos, own_sin = rope_tables((first + jnp.arange(rows, dtype=jnp.int32)).astype(jnp.float32))
    weight_q, weight_k, weight_v = (qkv_weight[:, index] for index in range(3))
    weight_kv = jnp.concatenate([weight_k, weight_v], axis=1)
    head_cols = weight_q.shape[1]
    heads = head_cols // HEAD_DIM
    pairs = heads // 2
    q = pack(
        matmul("td,dc->tc", hidden_own, weight_q),
        own_cos,
        own_sin,
        True,
        HEAD_DIM**-0.5 * LOG2E,
        LEFT,
    )

    pieces, outs, logs = [], [], []
    for index in range(CHUNKS):
        hidden = normalize(features(gathered[index]))[0] * gain_one
        offsets = jnp.arange(ctx_count, dtype=jnp.int32)[:, None] * rows + (
            index * piece + jnp.arange(piece, dtype=jnp.int32)[None, :]
        )
        cosine, sine = rope_tables(offsets.reshape(-1).astype(jnp.float32))
        k = pack(matmul("td,dc->tc", hidden, weight_k), cosine, sine, True, 1.0, RIGHT)
        v = pack(matmul("td,dc->tc", hidden, weight_v), cosine, sine, False, 1.0, RIGHT)
        out, log = attend(q, k, v)
        pieces.append((hidden, k, v, cosine, sine))
        outs.append(out)
        logs.append(log)
    most = functools.reduce(jnp.maximum, logs)
    shares = [jnp.exp2(log - most) for log in logs]
    total = sum(shares)
    attended = sum(out * share for out, share in zip(outs, shares)) / total
    lse = most + jnp.log2(total)

    residual = x_own + lax.psum(matmul("tc,cd->td", attended, attn_out_weight), "tensor")
    normed_two, inverse_two = normalize(residual)
    hidden_two = normed_two * gain_two
    a = matmul("td,df->tf", hidden_two, ff_in[:, 0])
    b = matmul("td,df->tf", hidden_two, ff_in[:, 1])
    c_full = features(c_half)
    dz = matmul("td,fd->tf", c_full, ff_out)
    gelu, gelu_pull = jax.vjp(lambda inner: jax.nn.gelu(inner, approximate=False), a)
    z = gelu * b
    da = gelu_pull(dz * b)[0]
    db = dz * gelu
    dh_two = lax.psum(
        matmul("tf,df->td", da, ff_in[:, 0]) + matmul("tf,df->td", db, ff_in[:, 1]), "tensor"
    )
    layer_out = own_features(residual) + lax.psum_scatter(
        matmul("tf,fd->td", z, ff_out), "tensor", scatter_dimension=1, tiled=True
    )
    scaled = dh_two * gain_two
    d_res = c_full + inverse_two * (
        scaled
        - jnp.mean(scaled, axis=-1, keepdims=True)
        - normed_two * jnp.mean(scaled * normed_two, axis=-1, keepdims=True)
    )

    out_grad_part = matmul("tf,td->fd", z, c_full)
    in_grad_part = jnp.stack(
        [matmul("td,tf->df", hidden_two, da), matmul("td,tf->df", hidden_two, db)], axis=1
    )
    attn_grad_part = matmul("tc,td->cd", attended, d_res)
    out_total, in_total, attn_total = lax.psum(
        (out_grad_part, in_grad_part, attn_grad_part), ("dp", "ctx")
    )

    do = matmul("td,cd->tc", d_res, attn_out_weight)
    delta = jnp.sum((do * attended).reshape(rows, heads, HEAD_DIM), axis=-1).T
    lse_rows = lse.reshape(rows, heads, HEAD_DIM)[:, :, 0].T
    stats = jnp.concatenate(
        [
            lse_rows.reshape(pairs, 2, rows),
            delta.reshape(pairs, 2, rows),
            jnp.zeros((pairs, 4, rows), jnp.float32),
        ],
        axis=1,
    )
    do_packed = pack(do, own_cos, own_sin, False, 1.0, LEFT)

    dq, dw_kv, dh_rows, earlier = None, None, [], None
    for hidden, k, v, cosine, sine in pieces:
        dk, dv, dq_part = attend_back(q, do_packed, k, v, stats, cosine, sine)
        dq = dq_part if dq is None else dq + dq_part
        dkv = jnp.concatenate([dk, dv], axis=1)
        dw_part = matmul("td,tc->dc", hidden, dkv)
        dw_kv = dw_part if dw_kv is None else dw_kv + dw_part
        dh_part = matmul("tc,dc->td", dkv, weight_kv)
        near = lax.psum_scatter(dh_part, "tensor", scatter_dimension=1, tiled=True)
        if earlier is not None:
            near, _ = lax.optimization_barrier((near, earlier))
        earlier = lax.psum_scatter(near, "ctx", scatter_dimension=0, tiled=True)
        dh_rows.append(earlier)

    dq = dq.reshape(heads, 2, HEAD_DIM // 2, rows) * HEAD_DIM**-0.5
    cos_t = own_cos[:, : HEAD_DIM // 2].T
    sin_t = own_sin[:, : HEAD_DIM // 2].T
    dq = jnp.stack(
        [dq[:, 0] * cos_t + dq[:, 1] * sin_t, dq[:, 1] * cos_t - dq[:, 0] * sin_t], axis=1
    ).reshape(head_cols, rows)
    dw_q = matmul("td,ct->dc", hidden_own, dq)
    dh_q = lax.psum_scatter(
        matmul("ct,dc->td", dq, weight_q), "tensor", scatter_dimension=1, tiled=True
    )
    qkv_part = jnp.stack([dw_q, dw_kv[:, :head_cols], dw_kv[:, head_cols:]], axis=1)
    qkv_part, in_total, out_total, attn_total = lax.optimization_barrier(
        (qkv_part, in_total, out_total, attn_total)
    )
    qkv_total = lax.psum(qkv_part, ("dp", "ctx"))

    gains = lax.psum_scatter(
        jnp.stack(
            [jnp.sum(qkv_weight * qkv_total, axis=(1, 2)), jnp.sum(ff_in * in_total, axis=(1, 2))]
        ),
        "tensor",
        scatter_dimension=1,
        tiled=True,
    )

    dh = jnp.concatenate(dh_rows, axis=0) + dh_q
    normed_half = own_features(normed_one)
    scaled = dh * attn_gain
    left, right = lax.psum(
        (
            jnp.sum(scaled, axis=-1, keepdims=True),
            jnp.sum(scaled * normed_half, axis=-1, keepdims=True),
        ),
        "tensor",
    )
    width = 2 * half
    input_grad = own_features(d_res) + inverse_one * (
        scaled - left / width - normed_half * right / width
    )
    return (
        layer_out[None],
        input_grad[None],
        gains[0] / attn_gain,
        qkv_total,
        attn_total,
        gains[1] / mlp_gain,
        in_total,
        out_total,
    )


def solution(mesh):
    rows = P("dp", "ctx", "tensor")
    in_specs = (
        rows,
        rows,
        P("tensor"),
        P(None, None, "tensor"),
        P("tensor", None),
        P("tensor"),
        P(None, None, "tensor"),
        P("tensor", None),
    )
    return jax.shard_map(
        body,
        mesh=mesh,
        in_specs=in_specs,
        out_specs=(rows, rows) + in_specs[2:],
        check_vma=False,
    )
```

time: 1960 us -> 1080 us (0.55)
  matrix products: 912 us -> 162 us
  Pallas kernels: 0 us -> 251 us
  waiting for transfers between devices: 687 us -> 515 us
  local copies, waits for them, and re-layouts: 133 us -> 58 us
  blocking collectives: 59.2 us -> 6.27 us
  other arithmetic: 110 us -> 62.3 us
  loops' own time: 30.3 us -> 0 us
    dot_general x96 -> x23, matrix products: 912 us -> 162 us  [matmul(): return jnp.einsum(spec, left, right, precision=PRECISION)]
    pallas_call x0 -> x10, Pallas kernels: none -> 251 us  [the longest x2 120 us: attend_back(): pl.pallas_call(functools.partial(attend_back_kernel, min(512, rows)), gri...]
    all_gather x6, waiting for transfers between devices: 231 us -> 142 us  [the longest x2 129 us: body(): far = lax.all_gather(part, 'ctx', axis=0, tiled=True)]
    psum x7 -> x1, blocking collectives: 59.2 us -> 2.5 us  [body(): lax.psum((jnp.sum(scaled, axis=-1, keepdims=True), jnp.sum(scaled * norme...]
    reduce_scatter x6, waiting for transfers between devices: 211 us -> 161 us  [the longest x2 127 us: body(): earlier = lax.psum_scatter(near, 'ctx', scatter_dimension=0, tiled=True)]
    psum x1 -> x4, waiting for transfers between devices: 245 us -> 201 us  [the longest x1 151 us: body(): qkv_total = lax.psum(qkv_part, ('dp', 'ctx'))]
    add x18 -> x4, other arithmetic: 38.5 us -> 7.22 us  [the longest x1 4.1 us: body(): lse = most + jnp.log2(total)]
    another operation x6 -> x0, loops' own time: 30.3 us -> none  [the longest x1 29.2 us: attend_sequence_back(): lax.scan(one_block, (empty, empty), (query_blocks(queries, rows), query_b...]
  transfers between devices with their start and end apart: 13 -> 17, of which waited for: 11 -> 14; matrix products, arithmetic and copies ran while one was open for 8% -> 15% of each run, Pallas kernels for 0% -> 12%
where the time goes in v1:
time: 1080 us; the launch traced here: 1070 us
  waiting for transfers between devices  515 us (48%)
  Pallas kernels  251 us (23%)
  matrix products  162 us (15%)
  other arithmetic  62.3 us (6%)
  local copies, waits for them, and re-layouts  58 us (5%)
  between operations  15.1 us (1%)
    dot_general x23, matrix products, matmul(): return jnp.einsum(spec, left, right, precision=PRECISION)  162 us
    psum x1, waiting for transfers between devices, body(): qkv_total = lax.psum(qkv_part, ('dp', 'ctx'))  151 us
    all_gather x2, waiting for transfers between devices, body(): far = lax.all_gather(part, 'ctx', axis=0, tiled=True)  129 us
    reduce_scatter x2, waiting for transfers between devices, body(): earlier = lax.psum_scatter(near, 'ctx', scatter_dimension=0, tiled=True)  127 us
    pallas_call x2, Pallas kernels, attend_back(): pl.pallas_call(functools.partial(attend_back_kernel, min(512, rows)), gri...  120 us
    pallas_call x2, Pallas kernels, attend(): pl.pallas_call(functools.partial(attend_kernel, min(1024, keys)), grid=(p...  77.8 us
    pallas_call x6, Pallas kernels, pack(): pl.pallas_call(functools.partial(pack_kernel, rotary, scale, order), grid...  53.3 us
    unnamed x132, local copies, waits for them, and re-layouts  34 us
  transfers between devices with their start and end apart: 17, of which 14 were waited for; matrix products, arithmetic and copies ran while one was open for 15% of the time, Pallas kernels for 12%

profile of v1, /device:TPU:0, one launch (start us, length us, event | category | flops | bytes accessed | tf_op | source)
XLA Modules:
  0.0 1070.9 jit_solution(858349920788480957)
XLA Ops:
  11.5 64.9 %all-gather.19.cloned.1.call-done = f32[1,2048,384]{2,1,0:T(8,128)} async-done(((f32[1,512,384]{2,1,0:T(8,128)}), f32[1,2048,384]{2,1,0:T(8,128)}) %all-gather.19.cloned.1.call-update) | async-done | bytes 3145744 | tf_op jit(solution)/shard_map/all_gather | solution.py:241
  76.5 64.2 %all-gather.13.cloned.1.call-done = f32[2048,384]{1,0:T(8,128)} async-done(((f32[512,384]{1,0:T(8,128)}), f32[2048,384]{1,0:T(8,128)}) %all-gather.13.cloned.1.call-update) | async-done | bytes 3145744 | tf_op jit(solution)/shard_map/all_gather | solution.py:241
  162.0 5.2 fusion.31.x_ref
  167.2 6.3 shard_map.143.q_ref
  180.2 11.6 %all-gather.15.cloned.1.call-done = f32[2048,768]{1,0:T(8,128)} async-done(((f32[2048,384]{1,0:T(8,128)}), f32[2048,768]{1,0:T(8,128)}) %all-gather.15.cloned.1.call-update) | async-done | bytes 6291472 | tf_op jit(solution)/shard_map/all_gather | solution.py:231
  195.0 3.7 multiply_reduce_fusion
  199.6 8.1 fusion.4.x_ref
  207.7 9.8 shard_map.148.v_ref
  217.5 8.8 fusion.5.x_ref
  226.3 11.3 %shard_map.147.k_ref = bf16[2048,1536]{1,0:T(8,128)(2,1)} custom-call(f32[2048,384]{1,0:T(8,128)} %fusion.5.x_ref, f32[2048,128]{1,0:T(8,128)} %copy.47.cos_ref, f32[2048,128]{1,0:T(8,128)} %copy.48.sin_ref), custom_call_target="tpu_custom_call" | custom-call | flops 6291456 | bytes 9437184 | tf_op jit(solution)/shard_map/pallas_call | solution.py:62
  237.7 8.1 fusion.1.x_ref
  245.7 9.7 shard_map.145.v_ref
  255.5 8.1 fusion.2.x_ref
  263.5 10.7 %shard_map.144.k_ref = bf16[2048,1536]{1,0:T(8,128)(2,1)} custom-call(f32[2048,384]{1,0:T(8,128)} %fusion.2.x_ref, f32[2048,128]{1,0:T(8,128)} %copy.43.cos_ref, f32[2048,128]{1,0:T(8,128)} %copy.44.sin_ref), custom_call_target="tpu_custom_call" | custom-call | flops 6291456 | bytes 9437184 | tf_op jit(solution)/shard_map/pallas_call | solution.py:62
  274.3 38.9 %shard_map.146 = (f32[1024,384]{1,0:T(8,128)}, f32[1024,384]{1,0:T(8,128)}) custom-call(bf16[1024,1536]{1,0:T(8,128)(2,1)} %shard_map.143.q_ref, bf16[2048,1536]{1,0:T(8,128)(2,1)} %shard_map.144.k_ref, bf16[2048,1536]{1,0:T(8,128)(2,1)} %shard_map.145.v_ref), custom_call_target="tpu_custom_call" | custom-call | flops 19327352832 | bytes 18874368 | tf_op jit(solution)/shard_map/pallas_call | solution.py:116
  313.2 38.9 %shard_map.149 = (f32[1024,384]{1,0:T(8,128)}, f32[1024,384]{1,0:T(8,128)}) custom-call(bf16[1024,1536]{1,0:T(8,128)(2,1)} %shard_map.143.q_ref, bf16[2048,1536]{1,0:T(8,128)(2,1)} %shard_map.147.k_ref, bf16[2048,1536]{1,0:T(8,128)(2,1)} %shard_map.148.v_ref), custom_call_target="tpu_custom_call" | custom-call | flops 19327352832 | bytes 18874368 | tf_op jit(solution)/shard_map/pallas_call | solution.py:116
  352.1 4.1 multiply_add_fusion.1
  356.2 4.3 fusion.93
  363.3 21.7 %all-reduce.7.cloned.1.call-done = f32[1024,768]{1,0:T(8,128)} async-done(((f32[1024,768]{1,0:T(8,128)}), f32[1024,768]{1,0:T(8,128)}) %all-reduce.7.cloned.1.call-update) | async-done | bytes 3145744 | tf_op jit(solution)/shard_map/psum | solution.py:280
  389.0 4.7 fusion.37
  393.7 4.7 fusion.39
  400.0 11.2 %multiply_add_fusion = (f32[1024,576]{0,1:T(8,128)S(1)}, f32[1024,576]{0,1:T(8,128)S(1)}, f32[1024,576]{0,1:T(8,128)S(1)}) fusion(f32[1024,576]{0,1:T(8,128)} %fusion.37, f32[1024,576]{0,1:T(8,128)} %fusion.39, f32[576,768]{1,0:T(8,128)S(1)} %copy-done, f32[1,1024,768]{2,1,0:T(8,128)} %all-gather.23.cloned.1.call-done), kind=kOutput, calls=%fused_computation.61 | convolution fusion | flops 2760376320 | bytes 16711680 | tf_op jit(solution)/shard_map/td,fd->tf/dot_general | solution.py:216
  415.7 4.2 fusion.51
  419.9 6.0 convolution_add_fusion
  433.6 6.3 fusion.66
  439.9 5.1 fusion.69
  449.5 4.4 fusion.6
  453.9 3.9 multiply_reduce_fusion.7
  466.6 6.5 fusion.92
  475.5 5.5 shard_map.150.do_ref
  481.7 59.8 %shard_map.151 = (f32[2048,384]{1,0:T(8,128)}, f32[2048,384]{1,0:T(8,128)}, f32[384,1024]{1,0:T(8,128)}) custom-call(bf16[1024,1536]{1,0:T(8,128)(2,1)} %shard_map.143.q_ref, bf16[1024,1536]{1,0:T(8,128)(2,1)} %shard_map.150.do_ref, bf16[2048,1536]{1,0:T(8,128)(2,1)} %shard_map.144.k_ref, bf16[2048,1536]{1,0:T(8,128)(2,1)} %shard_map.145.v_ref, ...), custom_call_target="tpu_custom_call" | custom-call | flops 51539607552 | bytes 18874368 | tf_op jit(solution)/shard_map/pallas_call | solution.py:186
  547.4 9.8 fusion.48
  558.3 60.3 %shard_map.152 = (f32[2048,384]{1,0:T(8,128)}, f32[2048,384]{1,0:T(8,128)}, f32[384,1024]{1,0:T(8,128)}) custom-call(bf16[1024,1536]{1,0:T(8,128)(2,1)} %shard_map.143.q_ref, bf16[1024,1536]{1,0:T(8,128)(2,1)} %shard_map.150.do_ref, bf16[2048,1536]{1,0:T(8,128)(2,1)} %shard_map.147.k_ref, bf16[2048,1536]{1,0:T(8,128)(2,1)} %shard_map.148.v_ref, ...), custom_call_target="tpu_custom_call" | custom-call | flops 51539607552 | bytes 18874368 | tf_op jit(solution)/shard_map/pallas_call | solution.py:186
  627.1 10.2 fusion
  637.4 9.9 fusion.65
  649.1 5.5 fusion.72
  656.7 28.3 %all-reduce.13.cloned.1.call-done = (f32[768,2,576]{0,2,1:T(8,128)}, f32[576,768]{1,0:T(8,128)}, f32[384,768]{1,0:T(8,128)}) async-done(((f32[768,2,576]{0,2,1:T(8,128)}, f32[576,768]{1,0:T(8,128)}, f32[384,768]{1,0:T(8,128)}), (f32[768,2,576]{0,2,1:T(8,128)}, f32[576,768]{1,0:T(8,128)}, f32[384,768]{1,0:T(8,128)})) %all-reduce.13.cloned.1.call-update) | async-done | bytes 6488080 | tf_op jit(solution)/shard_map/psum | solution.py:309
  685.1 12.4 %fusion.47 = f32[2048,768]{1,0:T(8,128)} fusion(f32[2048,768]{1,0:T(8,128)} %copy-done.30, f32[768,384]{1,0:T(8,128)} %get-tuple-element.57, f32[768,384]{1,0:T(8,128)} %get-tuple-element.56), kind=kOutput, calls=%fused_computation.76 | convolution fusion | flops 7248347136 | bytes 14942208 | tf_op jit(solution)/shard_map/tc,dc->td/dot_general | solution.py:216
  700.7 8.3 fusion.83
  712.6 151.3 %all-reduce.11.cloned.1.call-done = f32[768,3,384]{2,0,1:T(8,128)} async-done(((f32[768,3,384]{2,0,1:T(8,128)}), f32[768,3,384]{2,0,1:T(8,128)}) %all-reduce.11.cloned.1.call-update) | async-done | bytes 3538960 | tf_op jit(solution)/shard_map/psum | solution.py:354
  868.5 7.1 fusion.75
  875.7 3.9 reduce-scatter.16.cloned.1.call-done
  879.6 63.9 %reduce-scatter.14.cloned.1.call-done = f32[512,384]{1,0:T(8,128)} async-done(((f32[2048,384]{1,0:T(8,128)}), f32[512,384]{1,0:T(8,128)}) %reduce-scatter.14.cloned.1.call-update) | async-done | bytes 786448 | tf_op jit(solution)/shard_map/reduce_scatter | solution.py:337
  943.5 13.7 %reduce-scatter.10.cloned.1.call-done = f32[1024,384]{1,0:T(8,128)} async-done(((f32[1024,768]{1,0:T(8,128)}), f32[1024,384]{1,0:T(8,128)}) %reduce-scatter.10.cloned.1.call-update) | async-done | bytes 1572880 | tf_op jit(solution)/shard_map/reduce_scatter | solution.py:294
  960.3 8.5 reduce-scatter.22.cloned.1.call-done
  971.3 12.4 %reduce-scatter.20.cloned.1.call-done = f32[1024,384]{1,0:T(8,128)} async-done(((f32[1024,768]{1,0:T(8,128)}), f32[1024,384]{1,0:T(8,128)}) %reduce-scatter.20.cloned.1.call-update) | async-done | bytes 1572880 | tf_op jit(solution)/shard_map/reduce_scatter | solution.py:347
  983.7 63.6 %reduce-scatter.18.cloned.1.call-done = f32[512,384]{1,0:T(8,128)} async-done(((f32[2048,384]{1,0:T(8,128)}), f32[512,384]{1,0:T(8,128)}) %reduce-scatter.18.cloned.1.call-update) | async-done | bytes 786448 | tf_op jit(solution)/shard_map/reduce_scatter | solution.py:337
  1052.5 3.7 add_bitcast_fusion
  (249 shorter events, 122.6 us)
Async XLA Ops:
  7.2 392.8 %copy-start = (f32[576,768]{1,0:T(8,128)S(1)}, f32[576,768]{1,0:T(8,128)}, u32[]{:S(2)}) copy-start(f32[576,768]{1,0:T(8,128)} %param.15) | copy-start | bytes 5308420
  7.2 69.2 %all-gather.19.cloned.1.call-start = ((), (), s32[]{:S(2)}) async-start(), calls=%async_computation.19 | async-start | bytes 3932160 | tf_op jit(solution)/shard_map/all_gather | solution.py:241
  10.0 130.7 %all-gather.13.cloned.1.call-start = ((), (), s32[]{:S(2)}) async-start(), calls=%async_computation.7 | async-start | bytes 3932160 | tf_op jit(solution)/shard_map/all_gather | solution.py:241
  10.7 144.0 %all-gather.17.cloned.1.call-start = ((), (), s32[]{:S(2)}) async-start(), calls=%async_computation.18 | async-start | bytes 4718592 | tf_op jit(solution)/shard_map/all_gather | solution.py:231
  11.5 162.0 %all-gather.21.cloned.1.call-start = ((), (), s32[]{:S(2)}) async-start(), calls=%async_computation.20 | async-start | bytes 9437184 | tf_op jit(solution)/shard_map/all_gather | solution.py:231
  76.4 64.4 %copy-start.49 = (f32[384]{0:T(512)S(1)}, f32[384]{0:T(512)}, u32[]{:S(2)}) copy-start(f32[384]{0:T(512)} %param.10) | copy-start | bytes 4612
  76.4 115.4 %all-gather.15.cloned.1.call-start = ((), (), s32[]{:S(2)}) async-start(), calls=%async_computation.8 | async-start | bytes 9437184 | tf_op jit(solution)/shard_map/all_gather | solution.py:231
  140.7 244.3 %all-reduce.7.cloned.1.call-start = ((), (), s32[]{:S(2)}) async-start(), calls=%async_computation.9 | async-start | bytes 6291456 | tf_op jit(solution)/shard_map/psum | solution.py:280
  142.6 112.8 %copy-start.37 = (f32[768]{0:T(1024)}, f32[768]{0:T(1024)S(1)}, u32[]{:S(2)}) copy-start(f32[768]{0:T(1024)S(1)} %reshape.335) | copy-start | bytes 9220
  143.4 4.7 copy-start.24
  176.6 78.8 %copy-start.39 = (f32[2048]{0:T(1024)}, f32[2048]{0:T(1024)S(1)}, u32[]{:S(2)}) copy-start(f32[2048]{0:T(1024)S(1)} %broadcast_multiply_fusion.1) | copy-start | bytes 24580
  180.2 75.2 %copy-start.43 = (f32[2048]{0:T(1024)}, f32[2048]{0:T(1024)S(1)}, u32[]{:S(2)}) copy-start(f32[2048]{0:T(1024)S(1)} %add_rsqrt_fusion.1) | copy-start | bytes 24580
  194.9 22.5 %copy-start.41 = (f32[2048]{0:T(1024)}, f32[2048]{0:T(1024)S(1)}, u32[]{:S(2)}) copy-start(f32[2048]{0:T(1024)S(1)} %broadcast_multiply_fusion) | copy-start | bytes 24580
  199.6 17.9 %copy-start.45 = (f32[2048]{0:T(1024)}, f32[2048]{0:T(1024)S(1)}, u32[]{:S(2)}) copy-start(f32[2048]{0:T(1024)S(1)} %add_rsqrt_fusion) | copy-start | bytes 24580
  217.5 20.2 %slice-start = ((s8[6291456]{0:T(1024)(128)(4,1)}), s8[4194304]{0:T(1024)(128)(4,1)S(1)}, s32[]{:S(2)}) async-start(s8[6291456]{0:T(1024)(128)(4,1)} %bitcast.110), calls=%async_computation.24 | async-start | bytes 8388608
  226.3 11.3 %slice-start.1 = ((s8[6291456]{0:T(1024)(128)(4,1)}), s8[2097152]{0:T(1024)(128)(4,1)S(1)}, s32[]{:S(2)}) async-start(s8[6291456]{0:T(1024)(128)(4,1)} %bitcast.110), calls=%async_computation.25 | async-start | bytes 4194304
  313.1 38.9 %copy-start.28 = (f32[1024,384]{1,0:T(8,128)S(1)}, f32[1024,384]{1,0:T(8,128)}, u32[]{:S(2)}) copy-start(f32[1024,384]{1,0:T(8,128)} %get-tuple-element.24) | copy-start | bytes 4718596
  313.1 38.9 %copy-start.29 = (f32[1024,384]{1,0:T(8,128)S(1)}, f32[1024,384]{1,0:T(8,128)}, u32[]{:S(2)}) copy-start(f32[1024,384]{1,0:T(8,128)} %get-tuple-element.25) | copy-start | bytes 4718596
  360.5 39.5 %all-gather.23.cloned.1.call-start = ((), (), s32[]{:S(2)}) async-start(), calls=%async_computation.21 | async-start | bytes 4718592 | tf_op jit(solution)/shard_map/all_gather | solution.py:231
  361.2 92.7 %all-reduce.9.cloned.1.call-start = ((), (), s32[]{:S(2)}) async-start(), calls=%async_computation.11 | async-start | bytes 6291456 | tf_op jit(solution)/shard_map/psum | solution.py:291
  388.4 5.3 copy-start.1
  400.0 11.2 %copy-start.19 = (f32[1024,576]{0,1:T(8,128)S(1)}, f32[1024,576]{0,1:T(8,128)}, u32[]{:S(2)}) copy-start(f32[1024,576]{0,1:T(8,128)} %fusion.39) | copy-start | bytes 7077892
  411.2 8.7 copy-start.18
  412.0 8.0 copy-start.5
  426.0 259.0 %all-reduce.13.cloned.1.call-start = ((), (), s32[]{:S(2)}) async-start(), calls=%async_computation.23 | async-start | bytes 12976128 | tf_op jit(solution)/shard_map/psum | solution.py:309
  433.6 6.3 copy-start.2
  433.6 6.3 copy-start.6
  466.6 234.1 %reduce-scatter.12.cloned.1.call-start = ((), (), s32[]{:S(2)}) async-start(), calls=%async_computation.12 | async-start | bytes 9437184 | tf_op jit(solution)/shard_map/reduce_scatter | solution.py:334
  557.2 306.6 %all-reduce.11.cloned.1.call-start = ((), (), s32[]{:S(2)}) async-start(), calls=%async_computation.17 | async-start | bytes 7077888 | tf_op jit(solution)/shard_map/psum | solution.py:354
  558.3 60.3 %copy-start.33 = (f32[384,1024]{1,0:T(8,128)S(1)}, f32[384,1024]{1,0:T(8,128)}, u32[]{:S(2)}) copy-start(f32[384,1024]{1,0:T(8,128)} %get-tuple-element.34) | copy-start | bytes 4718596
  622.2 4.9 copy-start.32
  622.2 4.9 copy-start.38
  622.2 4.9 copy-start.40
  622.2 4.9 copy-start.44
  624.3 13.0 %slice-start.4 = ((s8[6291456]{0:T(1024)(128)(4,1)}), s8[4194304]{0:T(1024)(128)(4,1)S(1)}, s32[]{:S(2)}) async-start(s8[6291456]{0:T(1024)(128)(4,1)} %bitcast.114), calls=%async_computation.28 | async-start | bytes 8388608
  627.1 10.2 copy-start.30
  627.1 10.2 slice-start.5
  627.1 10.2 copy-start.42
  627.1 10.2 copy-start.46
  685.0 194.6 %reduce-scatter.16.cloned.1.call-start = ((), (), s32[]{:S(2)}) async-start(), calls=%async_computation.14 | async-start | bytes 9437184 | tf_op jit(solution)/shard_map/reduce_scatter | solution.py:334
  697.5 245.9 %reduce-scatter.14.cloned.1.call-start = ((), (), s32[]{:S(2)}) async-start(), calls=%async_computation.13 | async-start | bytes 3932160 | tf_op jit(solution)/shard_map/reduce_scatter | solution.py:337
  700.7 256.5 %reduce-scatter.10.cloned.1.call-start = ((), (), s32[]{:S(2)}) async-start(), calls=%async_computation.10 | async-start | bytes 4718592 | tf_op jit(solution)/shard_map/reduce_scatter | solution.py:294
  709.1 259.8 %reduce-scatter.22.cloned.1.call-start = ((), (), s32[]{:S(2)}) async-start(), calls=%async_computation.22 | async-start | bytes 589824
  868.3 115.4 %reduce-scatter.20.cloned.1.call-start = ((), (), s32[]{:S(2)}) async-start(), calls=%async_computation.16 | async-start | bytes 4718592 | tf_op jit(solution)/shard_map/reduce_scatter | solution.py:347
  875.6 171.7 %reduce-scatter.18.cloned.1.call-start = ((), (), s32[]{:S(2)}) async-start(), calls=%async_computation.15 | async-start | bytes 3932160 | tf_op jit(solution)/shard_map/reduce_scatter | solution.py:337
  943.5 26.6 %copy-start.52 = (f32[384]{0:T(512)S(1)}, f32[384]{0:T(512)}, u32[]{:S(2)}) copy-start(f32[384]{0:T(512)} %param.13) | copy-start | bytes 4612
  943.5 27.2 %copy-start.50 = (f32[384]{0:T(512)S(1)}, f32[384]{0:T(512)}, u32[]{:S(2)}) copy-start(f32[384]{0:T(512)} %param.10) | copy-start | bytes 4612
  971.3 81.2 %copy-start.48 = (f32[1024]{0:T(1024)S(1)}, f32[1024]{0:T(1024)}, u32[]{:S(2)}) copy-start(f32[1024]{0:T(1024)} %copy-done.47) | copy-start | bytes 12292
  (28 other events, 83.6 us)
Sparse Core Ops, SparseCore 0:
  10.2 66.1 all-gather.18
  78.5 62.1 all-gather.12
  142.3 10.7 all-gather.16
  154.5 17.9 all-gather.20
  173.8 17.9 all-gather.14
  360.6 24.3 all-reduce.6
  386.6 13.2 all-gather.22
  426.1 24.3 all-reduce.8
  466.7 218.2 all-reduce.12
  687.1 13.4 reduce-scatter.11
  708.0 155.7 all-reduce.10
  866.0 13.5 reduce-scatter.15
  882.0 61.4 reduce-scatter.13
  946.2 10.9 reduce-scatter.9
  959.8 8.9 reduce-scatter.21
  971.6 12.0 reduce-scatter.19
  985.8 61.3 reduce-scatter.17
